TPU v7x, 32 devices: a whole 2x2x4 slice. The times are simulated.
32 devices in a mesh: dp: 4 (over y, core), mp: 8 (over z, x).
Axes of the slice: x: 2, y: 2, z: 4, core: 2. Of those that a mesh axis runs over, the one named last changes fastest.
Arguments:
- tokens_in: bfloat16 [128, 8192], P('dp'), may hold values from -6 to 6
- gate_pre: bfloat16 [128, 28672], P('dp', 'mp'), may hold values from -6 to 6
- up_pre: bfloat16 [128, 28672], P('dp', 'mp'), may hold values from -6 to 6
- down_weight: bfloat16 [28672, 8192], P('mp', 'dp'), may hold values from -0.03125 to 0.03125
- slot_source: int32 [128], replicated, may hold values from 0 to 127, each once
- encoder: bfloat16 [8192, 32768], P('dp', 'mp'), may hold values from -0.0625 to 0.0625
- encoder_bias: float32 [32768], P('mp'), may hold values from -3 to 3
- decoder: bfloat16 [32768, 8192], P('mp', 'dp'), may hold values from -0.03125 to 0.03125
- decoder_bias: float32 [8192], P('dp'), may hold values from -3 to 3
Outputs:
- activations: bfloat16 [128, 32768], P('dp', 'mp')
- code_grad: float32 [128, 32768], P('dp', 'mp')
- decoder_grad: float32 [32768, 8192], P('mp', 'dp')
Inputs may be any that keep to these rules, and one draw needn't show every extreme that they name: Slot s of the shuffled batch takes harvested row slot_source[s]; every row fills exactly one slot.
All inputs are finite; a program needn't handle non-finite values.
Results may differ from a plain program's by a relative error of at most 0.015.
Values may be sent and summed in bfloat16 or wider, within the bound.
A program may use at most 192 MiB of HBM per device.

v0:
```python
import jax
import jax.numpy as jnp
from jax import lax
from jax.sharding import PartitionSpec as P


def on_device(
    tokens_in,
    gate_pre,
    up_pre,
    down_weight,
    slot_source,
    encoder,
    encoder_bias,
    decoder,
    decoder_bias,
):
    rows_here = tokens_in.shape[0]
    hidden = (jax.nn.silu(gate_pre.astype(jnp.float32)) * up_pre.astype(jnp.float32)).astype(
        jnp.bfloat16
    )
    target_part = jnp.dot(
        lax.all_gather(hidden, "dp", axis=0, tiled=True),
        down_weight,
        preferred_element_type=jnp.float32,
    )
    target_whole = lax.psum(target_part.astype(jnp.bfloat16), "mp").astype(jnp.float32)
    shuffled = jnp.take(target_whole, slot_source, axis=0)
    features = lax.all_to_all(tokens_in, "dp", split_axis=1, concat_axis=0, tiled=True)
    inputs = jnp.take(features, slot_source, axis=0)
    block = inputs
    preact_rows = lax.psum_scatter(
        jnp.dot(block, encoder, preferred_element_type=jnp.float32),
        "dp",
        scatter_dimension=0,
        tiled=True,
    )
    local_codes = jnp.maximum(preact_rows + encoder_bias, 0.0).astype(jnp.bfloat16)
    all_codes = lax.all_gather(local_codes, "dp", axis=0, tiled=True)
    rebuilt_part = jnp.dot(all_codes, decoder, preferred_element_type=jnp.float32)
    rebuilt = lax.psum(rebuilt_part.astype(jnp.bfloat16), "mp").astype(jnp.float32) + decoder_bias
    residual_grad = (rebuilt - shuffled).astype(jnp.bfloat16)
    block = residual_grad
    code_grad = lax.psum_scatter(
        lax.dot_general(
            block, decoder, (((1,), (1,)), ((), ())), preferred_element_type=jnp.float32
        ).astype(jnp.bfloat16),
        "dp",
        scatter_dimension=0,
        tiled=True,
    ).astype(jnp.float32)
    decoder_grad = (
        lax.dot_general(
            all_codes, residual_grad, (((0,), (0,)), ((), ())), preferred_element_type=jnp.float32
        )
        / rows_here
    )
    return (local_codes, code_grad, decoder_grad)


def solution(mesh):
    return jax.shard_map(
        on_device,
        mesh=mesh,
        in_specs=(
            P("dp", None),
            P("dp", "mp"),
            P("dp", "mp"),
            P("mp", "dp"),
            P(),
            P("dp", "mp"),
            P("mp"),
            P("mp", "dp"),
            P("dp"),
        ),
        out_specs=(P("dp", "mp"), P("dp", "mp"), P("mp", "dp")),
        check_vma=False,
    )
```

profile of v0, /device:TPU:0, one launch (start us, length us, event | category | flops | bytes accessed | tf_op | source)
XLA Modules:
  0.0 221.3 jit_solution(16659465956961364434)
XLA Ops:
  7.2 0.0 copy-start.3
  7.2 0.0 copy-start.1
  7.2 1.9 copy.15
  9.1 4.2 %all-to-all-start = ((bf16[32,4,2048]{2,0,1:T(8,128)(2,1)}), bf16[32,4,2048]{2,0,1:T(8,128)(2,1)S(1)}, u32[]{:S(2)}, u32[]{:S(2)}) async-start(bf16[32,4,2048]{2,0,1:T(8,128)(2,1)} %bitcast.15), calls=%async_computation | async-start | bytes 1048576 | tf_op jit(solution)/shard_map/all_to_all | solution.py:29
  13.4 0.7 compare_select_fusion
  14.0 0.7 compare_and_fusion
  14.7 7.5 %all-to-all-done = bf16[32,4,2048]{2,0,1:T(8,128)(2,1)S(1)} async-done(((bf16[32,4,2048]{2,0,1:T(8,128)(2,1)}), bf16[32,4,2048]{2,0,1:T(8,128)(2,1)S(1)}, u32[]{:S(2)}, u32[]{:S(2)}) %all-to-all-start) | async-done | bytes 524320 | tf_op jit(solution)/shard_map/all_to_all | solution.py:29
  22.2 0.9 gather_fusion
  23.2 9.5 %fusion = f32[128,4096]{1,0:T(8,128)} fusion(bf16[2048,4096]{1,0:T(8,128)(2,1)} %param.14, bf16[128,2048]{1,0:T(8,128)(2,1)S(1)} %gather_fusion, pred[128]{0:T(512)(128)(4,1)S(1)} %compare_and_fusion), kind=kOutput, calls=%fused_computation.11 | convolution fusion | flops 2147745792 | bytes 19398784 | tf_op jit(solution)/shard_map/dot_general | solution.py:33
  32.7 0.0 reduce-scatter.3.cloned.1.call-update
  32.7 0.0 all-gather.2.cloned.1.call-start
  32.7 32.5 %reduce-scatter.3.cloned.1.call-done = f32[32,4096]{1,0:T(8,128)} async-done(((f32[128,4096]{1,0:T(8,128)}), f32[32,4096]{1,0:T(8,128)}) %reduce-scatter.3.cloned.1.call-update) | async-done | bytes 524304 | tf_op jit(solution)/shard_map/reduce_scatter | solution.py:32
  65.2 1.8 maximum_convert_fusion
  67.0 0.0 all-gather.2.cloned.1.call-update
  67.0 0.0 all-reduce.3.cloned.1.call-start
  67.1 0.1 fusion.7
  67.2 8.9 %all_gather.7 = bf16[128,3584]{1,0:T(8,128)(2,1)S(1)} all-gather(bf16[32,3584]{1,0:T(8,128)(2,1)S(1)} %fusion.7), channel_id=1, replica_groups=mesh['dp'=4,'mp'=8] {'dp'}, dimensions={0}, use_global_device_ids=true | all-gather | bytes 1146880 | tf_op jit(solution)/shard_map/all_gather | solution.py:23
  76.1 8.3 %convolution_convert_fusion.1 = bf16[128,2048]{1,0:T(8,128)(2,1)} fusion(bf16[128,3584]{1,0:T(8,128)(2,1)S(1)} %all_gather.7, bf16[3584,2048]{1,0:T(8,128)(2,1)} %param.12), kind=kOutput, calls=%fused_computation.4 | convolution fusion | flops 1879310336 | bytes 16121856 | tf_op jit(solution)/shard_map/dot_general | solution.py:22
  84.5 9.2 %convolution_convert_fusion.2 = bf16[128,2048]{1,0:T(8,128)(2,1)} fusion(bf16[128,4096]{1,0:T(8,128)(2,1)} %all-gather.2.cloned.1.call-done, bf16[4096,2048]{1,0:T(8,128)(2,1)} %param.16), kind=kOutput, calls=%fused_computation.5 | convolution fusion | flops 2147745792 | bytes 18350080 | tf_op jit(solution)/shard_map/dot_general | solution.py:40
  93.7 0.0 all-reduce.3.cloned.1.call-update
  93.8 0.2 reduce-scatter.5.cloned.1.call-start
  94.0 78.7 %all-reduce.3.cloned.1.call-done = (bf16[128,2048]{1,0:T(8,128)(2,1)}, bf16[128,2048]{1,0:T(8,128)(2,1)}) async-done(((bf16[128,2048]{1,0:T(8,128)(2,1)}, bf16[128,2048]{1,0:T(8,128)(2,1)}), (bf16[128,2048]{1,0:T(8,128)(2,1)}, bf16[128,2048]{1,0:T(8,128)(2,1)})) %all-reduce.3.cloned.1.call-update) | async-done | bytes 1048592 | tf_op jit(solution)/shard_map/psum | solution.py:27
  172.7 1.1 convert_element_type.40
  173.9 1.0 gather_fusion.1
  174.8 0.0 copy-done.4
  174.9 1.2 subtract_convert_fusion
  176.1 12.4 %convolution_convert_fusion = bf16[128,4096]{1,0:T(8,128)(2,1)} fusion(bf16[128,2048]{1,0:T(8,128)(2,1)S(1)} %subtract_convert_fusion, bf16[4096,2048]{1,0:T(8,128)(2,1)} %param.16), kind=kOutput, calls=%fused_computation.3 | convolution fusion | flops 2148007936 | bytes 18350080 | tf_op jit(solution)/shard_map/dot_general | solution.py:45
  188.5 0.0 reduce-scatter.5.cloned.1.call-update
  188.5 0.0 copy-done
  188.5 14.1 %broadcast_multiply_fusion = f32[4096,2048]{1,0:T(8,128)} fusion(bf16[128,4096]{1,0:T(8,128)(2,1)S(1)} %copy-done, bf16[128,2048]{1,0:T(8,128)(2,1)S(1)} %subtract_convert_fusion), kind=kOutput, calls=%fused_computation.2 | convolution fusion | flops 2155872256 | bytes 35127296 | tf_op jit(solution)/shard_map/dot_general | solution.py:53
  202.6 10.4 %reduce-scatter.5.cloned.1.call-done = bf16[32,4096]{1,0:T(8,128)(2,1)} async-done(((bf16[128,4096]{1,0:T(8,128)(2,1)}), bf16[32,4096]{1,0:T(8,128)(2,1)}) %reduce-scatter.5.cloned.1.call-update) | async-done | bytes 262160 | tf_op jit(solution)/shard_map/reduce_scatter | solution.py:44
  213.0 1.8 convert_element_type.43
  (9 shorter events, 0.0 us)
Async XLA Ops:
  7.2 58.0 %copy-start.3 = (f32[4096]{0:T(1024)S(1)}, f32[4096]{0:T(1024)}, u32[]{:S(2)}) copy-start(f32[4096]{0:T(1024)} %param.15) | copy-start | bytes 49156
  7.2 59.9 %copy-start.1 = (bf16[32,3584]{1,0:T(8,128)(2,1)S(1)}, bf16[32,3584]{1,0:T(8,128)(2,1)}, u32[]{:S(2)}) copy-start(bf16[32,3584]{1,0:T(8,128)(2,1)} %param.11) | copy-start | bytes 688132
  7.2 59.9 %copy-start.2 = (bf16[32,3584]{1,0:T(8,128)(2,1)S(1)}, bf16[32,3584]{1,0:T(8,128)(2,1)}, u32[]{:S(2)}) copy-start(bf16[32,3584]{1,0:T(8,128)(2,1)} %param.10) | copy-start | bytes 688132
  9.1 13.1 %all-to-all-start = ((bf16[32,4,2048]{2,0,1:T(8,128)(2,1)}), bf16[32,4,2048]{2,0,1:T(8,128)(2,1)S(1)}, u32[]{:S(2)}, u32[]{:S(2)}) async-start(bf16[32,4,2048]{2,0,1:T(8,128)(2,1)} %bitcast.15), calls=%async_computation | async-start | bytes 1048576 | tf_op jit(solution)/shard_map/all_to_all | solution.py:29
  13.4 51.8 %reduce-scatter.3.cloned.1.call-start = ((), (), s32[]{:S(2)}) async-start(), calls=%async_computation.3 | async-start | bytes 2621440 | tf_op jit(solution)/shard_map/reduce_scatter | solution.py:32
  32.7 51.8 %all-gather.2.cloned.1.call-start = ((), (), s32[]{:S(2)}) async-start(), calls=%async_computation.4 | async-start | bytes 1310720 | tf_op jit(solution)/shard_map/all_gather | solution.py:39
  67.0 105.7 %all-reduce.3.cloned.1.call-start = ((), (), s32[]{:S(2)}) async-start(), calls=%async_computation.6 | async-start | bytes 2097152 | tf_op jit(solution)/shard_map/psum | solution.py:27
  84.5 90.4 %copy-start.4 = (f32[2048]{0:T(1024)S(1)}, f32[2048]{0:T(1024)}, u32[]{:S(2)}) copy-start(f32[2048]{0:T(1024)} %param.17) | copy-start | bytes 24580
  93.7 94.8 %copy-start = (bf16[128,4096]{1,0:T(8,128)(2,1)S(1)}, bf16[128,4096]{1,0:T(8,128)(2,1)}, u32[]{:S(2)}) copy-start(bf16[128,4096]{1,0:T(8,128)(2,1)} %all-gather.2.cloned.1.call-done) | copy-start | bytes 3145732
  93.8 119.2 %reduce-scatter.5.cloned.1.call-start = ((), (), s32[]{:S(2)}) async-start(), calls=%async_computation.5 | async-start | bytes 1310720 | tf_op jit(solution)/shard_map/reduce_scatter | solution.py:44
Sparse Core Ops, SparseCore 0:
  32.8 32.3 reduce-scatter.2
  67.4 16.7 all-gather.1
  93.9 78.7 all-reduce.2
  188.6 24.2 reduce-scatter.4
where the time goes:
time: 222 us; the launch traced here: 221 us
  waiting for transfers between devices  129 us (58%)
  matrix products  53.6 us (24%)
  between operations  13.8 us (6%)
  blocking collectives  8.93 us (4%)
  other arithmetic  7.38 us (3%)
  starting transfers between devices  4.54 us (2%)
  local copies, waits for them, and re-layouts  3.86 us (2%)
    psum x1, waiting for transfers between devices, on_device(): lax.psum(target_part.astype(jnp.bfloat16), 'mp').astype(jnp.float32)  78.7 us
    reduce_scatter x1, waiting for transfers between devices, on_device(): lax.psum_scatter(jnp.dot(block, encoder, preferred_element_type=jnp.float...  32.5 us
    dot_general x1, matrix products, on_device(): lax.dot_general(all_codes, residual_grad, (((0,), (0,)), ((), ())), prefe...  14.1 us
    dot_general x1, matrix products, on_device(): lax.dot_general(block, decoder, (((1,), (1,)), ((), ())), preferred_eleme...  12.4 us
    reduce_scatter x1, waiting for transfers between devices, on_device(): lax.psum_scatter(lax.dot_general(block, decoder, (((1,), (1,)), ((), ()))...  10.4 us
    dot_general x1, matrix products, on_device(): jnp.dot(block, encoder, preferred_element_type=jnp.float32)  9.5 us
    dot_general x1, matrix products, on_device(): jnp.dot(all_codes, decoder, preferred_element_type=jnp.float32)  9.25 us
    all_gather x1, blocking collectives, on_device(): lax.all_gather(hidden, 'dp', axis=0, tiled=True)  8.93 us
  transfers between devices with their start and end apart: 5, of which 4 were waited for; matrix products, arithmetic and copies ran while one was open for 11% of the time, Pallas kernels for 0%

commit v1 on v0

v1 whole, which is shorter than its diff:
```python
import functools

import jax
import jax.numpy as jnp
from jax import lax
from jax.experimental import pallas as pl
from jax.experimental.pallas import tpu as pltpu
from jax.sharding import PartitionSpec as P

MESH = pl.DeviceIdType.MESH
F32 = jnp.float32
BF16 = jnp.bfloat16
MIB = 1 << 20
CHUNKS = 4
HALVES = 2


def forward(
    sizes,
    slot_ref,
    tok_ref,
    gate_ref,
    up_ref,
    down_hbm,
    enc_hbm,
    eb_ref,
    dec_hbm,
    db_ref,
    act_out,
    cg_out,
    codes_out,
    res_out,
    enc,
    dec,
    down,
    tok_in,
    x,
    hid,
    hperm,
    part,
    psend,
    crecv,
    ysend,
    yrecv,
    codes,
    acc,
    ssend,
    xrecv,
    zsum,
    zsend,
    zrecv,
    res,
    send_sem,
    recv_sem,
    local_sem,
):
    dp, pairs, inner, outer, rows_here, cw, sw, tile, stile = sizes
    rows = dp * rows_here
    width = acc.shape[1]
    r16 = rows // (inner * outer)
    d = lax.axis_index("dp")
    m = lax.axis_index("mp")
    q, c = d // 2, lax.rem(d, 2)
    b, a = m // inner, lax.rem(m, inner)
    partner = 2 * q + 1 - c

    counter = [0, 0]

    def send(src, dst, **where):
        i = counter[0]
        counter[0] += 1
        copy = pltpu.make_async_remote_copy(
            src_ref=src,
            dst_ref=dst,
            send_sem=send_sem.at[i],
            recv_sem=recv_sem.at[i],
            device_id=where,
            device_id_type=MESH,
        )
        copy.start()
        return copy

    def local(src, dst):
        i = counter[1]
        counter[1] += 1
        copy = pltpu.make_async_copy(src, dst, local_sem.at[i])
        copy.start()
        return copy

    def at_chunk(k):
        return pl.ds(k * cw, cw)

    tok_own = local(tok_ref.at[:, pl.ds(pl.multiple_of(d * width, 128), width)], tok_in.at[d])
    enc_loads = [local(enc_hbm.at[:, at_chunk(k)], enc.at[k]) for k in range(CHUNKS)]
    down_load = local(down_hbm, down)
    dec_loads = [local(dec_hbm.at[at_chunk(k)], dec.at[at_chunk(k)]) for k in range(CHUNKS)]

    barrier = pltpu.get_barrier_semaphore()
    for i in range(1, dp):
        pl.semaphore_signal(
            barrier, inc=1, device_id={"dp": lax.rem(d + i, dp)}, device_id_type=MESH
        )
    for i in range(1, inner):
        pl.semaphore_signal(
            barrier,
            inc=1,
            device_id={"mp": b * inner + lax.rem(a + i, inner)},
            device_id_type=MESH,
        )
    for i in range(1, outer):
        pl.semaphore_signal(
            barrier,
            inc=1,
            device_id={"mp": lax.rem(b + i, outer) * inner + a},
            device_id_type=MESH,
        )
    pl.semaphore_wait(barrier, dp - 1 + inner - 1 + outer - 1)

    def same_core(i):
        return 2 * lax.rem(q + i, pairs) + c

    def gather_start(here):
        far = [send(here.at[d], here.at[d], dp=same_core(i)) for i in range(1, pairs)]
        near = send(here.at[d], here.at[d], dp=partner)
        return far, near

    def gather_pass(here, far):
        passed = []
        for i, copy in enumerate(far, 1):
            copy.wait_recv()
            came = 2 * lax.rem(q + pairs - i, pairs) + c
            passed.append(send(here.at[came], here.at[came], dp=partner))
        return passed

    tok_copies = []
    for i in range(1, dp):
        peer = lax.rem(d + i, dp)
        cols = pl.ds(pl.multiple_of(peer * width, 128), width)
        tok_copies.append(send(tok_ref.at[:, cols], tok_in.at[d], dp=peer))
    gate = gate_ref[...].astype(F32)
    hid[d] = (gate / (1.0 + jnp.exp(-gate)) * up_ref[...].astype(F32)).astype(BF16)
    hid_far, hid_near = gather_start(hid)

    pick = (slot_ref[...] == lax.broadcasted_iota(jnp.int32, (rows, rows), 1)).astype(F32)
    pick = pick.astype(BF16)

    tok_own.wait()
    for copy in tok_copies:
        copy.wait_recv()
    x[...] = jnp.dot(pick, tok_in[...].reshape(rows, width), preferred_element_type=F32).astype(
        BF16
    )

    def part_store(k, cols, value):
        value = value.reshape(dp, rows_here, value.shape[1])
        part[k, :, :, cols] = value
        psend[k, :, :, :, cols] = value.astype(BF16).reshape((pairs, 2) + value.shape[1:])

    def encode(k):
        enc_loads[k].wait()

        @pl.loop(0, cw // tile)
        def _(t):
            cols = pl.ds(pl.multiple_of(t * tile, tile), tile)
            part_store(k, cols, jnp.dot(x[...], enc[k, :, cols], preferred_element_type=F32))

        return send(psend.at[k, :, 1 - c], crecv.at[k], dp=partner)

    def pair_sum(k, core_copy):
        core_copy.wait_recv()
        for j in range(pairs):
            total = part[k, 2 * j + c] + crecv[k, j].astype(F32)
            part[k, 2 * j + c] = total
            ysend[k, j] = total.astype(BF16)
        return [
            send(ysend.at[k, lax.rem(q + i, pairs)], yrecv.at[k, i - 1], dp=same_core(i))
            for i in range(1, pairs)
        ]

    def far_sum(k, far_copies):
        total = part[k, d]
        for i, copy in enumerate(far_copies):
            copy.wait_recv()
            total = total + yrecv[k, i].astype(F32)
        return total

    def activate(k, far_copies):
        codes[k, d] = jnp.maximum(far_sum(k, far_copies) + eb_ref[:, at_chunk(k)], 0.0).astype(
            BF16
        )
        outs.append(local(codes.at[k, d], act_out.at[:, at_chunk(k)]))
        return gather_start(codes.at[k])

    def decode(k, near, passed, cols):
        for copy in [near] + passed:
            copy.wait_recv()
        outs.append(local(codes.at[k], codes_out.at[k]))
        dec_loads[k].wait()

        @pl.loop(0, width // tile)
        def _(t):
            cols = pl.ds(pl.multiple_of(t * tile, tile), tile)
            acc[:, cols] += jnp.dot(
                codes[k].reshape(rows, cw), dec[at_chunk(k), cols], preferred_element_type=F32
            )

    outs, sends = [], []
    core, far, gathers = {}, {}, {}
    for k in range(CHUNKS):
        core[k] = encode(k)
        if k >= 1:
            far[k - 1] = pair_sum(k - 1, core[k - 1])
    far[CHUNKS - 1] = pair_sum(CHUNKS - 1, core[CHUNKS - 1])

    hid_passed = gather_pass(hid, hid_far)
    gathers[0] = activate(0, far[0])
    for copy in [hid_near] + hid_passed:
        copy.wait_recv()
    hperm[...] = jnp.dot(
        pick, hid[...].reshape(rows, hid.shape[2]), preferred_element_type=F32
    ).astype(BF16)
    down_load.wait()
    passes = {}
    steps = width // tile
    for k in range(CHUNKS):

        @pl.loop(k * steps // CHUNKS, (k + 1) * steps // CHUNKS)
        def _(t):
            cols = pl.ds(pl.multiple_of(t * tile, tile), tile)
            acc[:, cols] = -jnp.dot(hperm[...], down[:, cols], preferred_element_type=F32)

        if k + 1 < CHUNKS:
            gathers[k + 1] = activate(k + 1, far[k + 1])
        passes[k] = gather_pass(codes.at[k], gathers[k][0])
    for k in range(CHUNKS - 1):
        decode(k, gathers[k][1], passes[k], None)

    last = CHUNKS - 1
    for copy in [gathers[last][1]] + passes[last]:
        copy.wait_recv()
    outs.append(local(codes.at[last], codes_out.at[last]))
    dec_loads[last].wait()

    def split_sum(s):
        @pl.loop(0, sw // stile)
        def _(t):
            there = pl.ds(pl.multiple_of(t * stile, stile), stile)
            cols = pl.ds(pl.multiple_of(s * sw + t * stile, stile), stile)
            total = acc[:, cols] + jnp.dot(
                codes[last].reshape(rows, cw), dec[at_chunk(last), cols], preferred_element_type=F32
            )
            acc[:, cols] = total
            ssend[s, :, :, :, there] = total.astype(BF16).reshape(inner, outer, r16, stile)

        return [
            send(
                ssend.at[s, lax.rem(a + i, inner)],
                xrecv.at[s, i - 1],
                mp=b * inner + lax.rem(a + i, inner),
            )
            for i in range(1, inner)
        ]

    def inner_sum(s, copies):
        own = pl.ds(pl.multiple_of(a * (outer * r16), outer * r16), outer * r16)
        total = acc[own, s * sw : (s + 1) * sw].reshape(outer, r16, sw)
        for i, copy in enumerate(copies):
            copy.wait_recv()
            total = total + xrecv[s, i].astype(F32)
        zsum[s] = total
        zsend[s] = total.astype(BF16)
        return [
            send(
                zsend.at[s, lax.rem(b + i, outer)],
                zrecv.at[s, i - 1],
                mp=lax.rem(b + i, outer) * inner + a,
            )
            for i in range(1, outer)
        ]

    def outer_sum(s, copies):
        total = zsum[s, b]
        for i, copy in enumerate(copies):
            copy.wait_recv()
            total = total + zrecv[s, i].astype(F32)
        res[s, a, b] = (total + db_ref[:, s * sw : (s + 1) * sw]).astype(BF16)
        return [
            send(res.at[s, a, b], res.at[s, a, b], mp=lax.rem(b + i, outer) * inner + a)
            for i in range(1, outer)
        ]

    def inner_gather(s, copies):
        for copy in copies:
            copy.wait_recv()
        return [
            send(res.at[s, a], res.at[s, a], mp=b * inner + lax.rem(a + i, inner))
            for i in range(1, inner)
        ]

    first = [split_sum(s) for s in range(HALVES)]
    second = [inner_sum(s, first[s]) for s in range(HALVES)]
    third = [outer_sum(s, second[s]) for s in range(HALVES)]
    fourth = [inner_gather(s, third[s]) for s in range(HALVES)]

    for k in range(CHUNKS):
        for copy in [core[k]] + far[k]:
            copy.wait_send()
    back, back_far = {}, {}
    for s in range(HALVES):
        for copy in fourth[s]:
            copy.wait_recv()
        outs.append(local(res.at[s], res_out.at[s]))
        for k in range(CHUNKS):

            @pl.loop(0, cw // tile)
            def _(t):
                cols = pl.ds(pl.multiple_of(t * tile, tile), tile)
                hidden_rows = pl.ds(pl.multiple_of(k * cw + t * tile, tile), tile)
                value = lax.dot_general(
                    res[s].reshape(rows, sw),
                    dec[hidden_rows, s * sw : (s + 1) * sw],
                    (((1,), (1,)), ((), ())),
                    preferred_element_type=F32,
                )
                if s > 0:
                    value = value + part[k, :, :, cols].reshape(rows, tile)
                if s < HALVES - 1:
                    part[k, :, :, cols] = value.reshape(dp, rows_here, tile)
                else:
                    part_store(k, cols, value)

            if s == HALVES - 1:
                back[k] = send(psend.at[k, :, 1 - c], crecv.at[k], dp=partner)
                if k >= 1:
                    back_far[k - 1] = pair_sum(k - 1, back[k - 1])
    back_far[last] = pair_sum(last, back[last])
    for k in range(CHUNKS):
        cg_out[:, at_chunk(k)] = far_sum(k, back_far[k])

    for copy in tok_copies + hid_far + [hid_near] + hid_passed:
        copy.wait_send()
    for k in range(CHUNKS):
        for copy in gathers[k][0] + [gathers[k][1]] + passes[k] + [back[k]] + back_far[k]:
            copy.wait_send()
    for s in range(HALVES):
        for copy in first[s] + second[s] + third[s] + fourth[s]:
            copy.wait_send()
    for copy in outs:
        copy.wait()


def decoder_gradient(scale, codes_ref, res_ref, out_ref):
    rows = codes_ref.shape[0] * codes_ref.shape[1]
    columns = res_ref.shape[2]
    for s in range(res_ref.shape[0]):
        out_ref[:, s * columns : (s + 1) * columns] = (
            lax.dot_general(
                codes_ref[...].reshape(rows, codes_ref.shape[2]),
                res_ref[s],
                (((0,), (0,)), ((), ())),
                preferred_element_type=F32,
            )
            * scale
        )


def on_device(
    dp,
    mp,
    tokens_in,
    gate_pre,
    up_pre,
    down_weight,
    slot_source,
    encoder,
    encoder_bias,
    decoder,
    decoder_bias,
):
    rows_here = tokens_in.shape[0]
    rows = rows_here * dp
    width, features = encoder.shape
    units = down_weight.shape[0]
    pairs = dp // 2
    inner = 1 << ((mp.bit_length() - 1) // 2)
    outer = mp // inner
    r16 = rows // mp
    cw, sw = features // CHUNKS, width // HALVES
    tile, stile = min(256, cw, width), min(256, sw)
    far = max(pairs - 1, 1)
    copies = (dp - 1) + 2 * pairs - 1 + CHUNKS * (1 + pairs - 1 + 2 * pairs - 1)
    copies += HALVES * 2 * (inner - 1 + outer - 1) + CHUNKS * pairs
    locals_ = 1 + CHUNKS + 1 + CHUNKS + 2 * CHUNKS + HALVES
    vmem = pl.BlockSpec(memory_space=pltpu.VMEM)
    anywhere = pl.BlockSpec(memory_space=pl.ANY)
    local_codes, code_grad, codes, res = pl.pallas_call(
        functools.partial(
            forward, (dp, pairs, inner, outer, rows_here, cw, sw, tile, stile)
        ),
        out_shape=(
            jax.ShapeDtypeStruct((rows_here, features), BF16),
            jax.ShapeDtypeStruct((rows_here, features), F32),
            jax.ShapeDtypeStruct((CHUNKS, dp, rows_here, cw), BF16),
            jax.ShapeDtypeStruct((HALVES, inner, outer, r16, sw), BF16),
        ),
        in_specs=[vmem, anywhere, vmem, vmem, anywhere, anywhere, vmem, anywhere, vmem],
        out_specs=(anywhere, vmem, anywhere, anywhere),
        scratch_shapes=[
            pltpu.VMEM((CHUNKS, width, cw), BF16),
            pltpu.VMEM((features, width), BF16),
            pltpu.VMEM((units, width), BF16),
            pltpu.VMEM((dp, rows_here, width), BF16),
            pltpu.VMEM((rows, width), BF16),
            pltpu.VMEM((dp, rows_here, units), BF16),
            pltpu.VMEM((rows, units), BF16),
            pltpu.VMEM((CHUNKS, dp, rows_here, cw), F32),
            pltpu.VMEM((CHUNKS, pairs, 2, rows_here, cw), BF16),
            pltpu.VMEM((CHUNKS, pairs, rows_here, cw), BF16),
            pltpu.VMEM((CHUNKS, pairs, rows_here, cw), BF16),
            pltpu.VMEM((CHUNKS, far, rows_here, cw), BF16),
            pltpu.VMEM((CHUNKS, dp, rows_here, cw), BF16),
            pltpu.VMEM((rows, width), F32),
            pltpu.VMEM((HALVES, inner, outer, r16, sw), BF16),
            pltpu.VMEM((HALVES, max(inner - 1, 1), outer, r16, sw), BF16),
            pltpu.VMEM((HALVES, outer, r16, sw), F32),
            pltpu.VMEM((HALVES, outer, r16, sw), BF16),
            pltpu.VMEM((HALVES, max(outer - 1, 1), r16, sw), BF16),
            pltpu.VMEM((HALVES, inner, outer, r16, sw), BF16),
            pltpu.SemaphoreType.DMA((copies,)),
            pltpu.SemaphoreType.DMA((copies,)),
            pltpu.SemaphoreType.DMA((locals_,)),
        ],
        compiler_params=pltpu.CompilerParams(
            collective_id=0, has_side_effects=True, vmem_limit_bytes=62 * MIB
        ),
        cost_estimate=pl.CostEstimate(
            flops=2 * rows * width * (2 * features + units) + 2 * rows * width * features,
            bytes_accessed=2 * width * (2 * features + units),
            transcendentals=0,
        ),
        name="forward",
    )(
        slot_source.reshape(rows, 1),
        tokens_in,
        gate_pre,
        up_pre,
        down_weight,
        encoder,
        encoder_bias.reshape(1, features),
        decoder,
        decoder_bias.reshape(1, width),
    )

    block = min(256, cw)
    per = cw // block
    decoder_grad = pl.pallas_call(
        functools.partial(decoder_gradient, 1.0 / rows_here),
        grid=(features // block,),
        out_shape=jax.ShapeDtypeStruct((features, width), F32),
        in_specs=[
            pl.BlockSpec((None, dp, rows_here, block), lambda f: (f // per, 0, 0, f % per)),
            pl.BlockSpec((HALVES, rows, sw), lambda f: (0, 0, 0)),
        ],
        out_specs=pl.BlockSpec((block, width), lambda f: (f, 0)),
        compiler_params=pltpu.CompilerParams(vmem_limit_bytes=32 * MIB),
        cost_estimate=pl.CostEstimate(
            flops=2 * rows * width * features,
            bytes_accessed=4 * width * features,
            transcendentals=0,
        ),
        name="decoder_gradient",
    )(codes, res.reshape(HALVES, rows, sw))
    return (local_codes, code_grad, decoder_grad)


def solution(mesh):
    return jax.shard_map(
        functools.partial(on_device, mesh.shape["dp"], mesh.shape["mp"]),
        mesh=mesh,
        in_specs=(
            P("dp", None),
            P("dp", "mp"),
            P("dp", "mp"),
            P("mp", "dp"),
            P(),
            P("dp", "mp"),
            P("mp"),
            P("mp", "dp"),
            P("dp"),
        ),
        out_specs=(P("dp", "mp"), P("dp", "mp"), P("mp", "dp")),
        check_vma=False,
    )
```

time: 222 us -> 96.4 us (0.43)
  waiting for transfers between devices: 129 us -> 0 us
  Pallas kernels: 0 us -> 90.4 us
  matrix products: 53.6 us -> 0 us
  between operations: 13.8 us -> 0.65 us
  blocking collectives: 8.93 us -> 0 us
  other arithmetic: 7.38 us -> 0 us
  starting transfers between devices: 4.54 us -> 0 us
    pallas_call x0 -> x2, Pallas kernels: none -> 90.4 us  [the longest x1 75.3 us: on_device(): pl.pallas_call(functools.partial(forward, (dp, pairs, inner, outer, rows_...]
    psum x1 -> x0, waiting for transfers between devices: 78.7 us -> none  [on_device(): lax.psum(target_part.astype(jnp.bfloat16), 'mp').astype(jnp.float32)]
    dot_general x5 -> x0, matrix products: 53.6 us -> none  [the longest x1 14.1 us: on_device(): lax.dot_general(all_codes, residual_grad, (((0,), (0,)), ((), ())), prefe...]
    reduce_scatter x2 -> x0, waiting for transfers between devices: 42.8 us -> none  [the longest x1 32.5 us: on_device(): lax.psum_scatter(jnp.dot(block, encoder, preferred_element_type=jnp.float...]
    all_gather x1 -> x0, blocking collectives: 8.93 us -> none  [on_device(): lax.all_gather(hidden, 'dp', axis=0, tiled=True)]
    all_to_all x1 -> x0, waiting for transfers between devices: 7.52 us -> none  [on_device(): lax.all_to_all(tokens_in, 'dp', split_axis=1, concat_axis=0, tiled=True)]
    convert_element_type x5 -> x0, other arithmetic: 6.06 us -> none  [the longest x1 1.79 us: on_device(): jnp.maximum(preact_rows + encoder_bias, 0.0).astype(jnp.bfloat16)]
    all_to_all x1 -> x0, starting transfers between devices: 4.24 us -> none  [on_device(): lax.all_to_all(tokens_in, 'dp', split_axis=1, concat_axis=0, tiled=True)]
  transfers between devices with their start and end apart: 5 -> 0, of which waited for: 4 -> 0; matrix products, arithmetic and copies ran while one was open for 11% -> 0% of each run, Pallas kernels for 0% -> 0%
where the time goes in v1:
time: 96.4 us; the launch traced here: 96.2 us
  Pallas kernels  90.4 us (94%)
  local copies, waits for them, and re-layouts  5.15 us (5%)
    pallas_call x1, Pallas kernels, on_device(): pl.pallas_call(functools.partial(forward, (dp, pairs, inner, outer, rows_...  75.3 us
    pallas_call x1, Pallas kernels, on_device(): pl.pallas_call(functools.partial(decoder_gradient, 1.0 / rows_here), grid...  15 us
    unnamed x10, local copies, waits for them, and re-layouts  3.76 us

profile of v1, /device:TPU:0, one launch (start us, length us, event | category | flops | bytes accessed | tf_op | source)
XLA Modules:
  0.0 96.2 jit_solution(4418430011102470768)
XLA Ops:
  0.6 1.4 %copy.12.slot_ref = s32[128,1]{1,0:T(8,128)} copy(s32[128,1]{0,1:T(1,128)} %bitcast.7) | data formatting | bytes 1024 | tf_op jit(solution)/shard_map/reshape | solution.py:443
  2.0 75.3 %forward.1 = (bf16[32,4096]{1,0:T(8,128)(2,1)}, f32[32,4096]{1,0:T(8,128)}, bf16[4,4,32,1024]{3,2,1,0:T(8,128)(2,1)}, bf16[2,2,4,16,1024]{4,3,2,1,0:T(8,128)(2,1)}) custom-call(s32[128,1]{1,0:T(8,128)} %copy.12.slot_ref, bf16[32,8192]{1,0:T(8,128)(2,1)} %tok_ref.1, bf16[32,3584]{1,0:T(8,128)(2,1)} %gate_ref.1, bf16[32,3584]{1,0:T(8,128)(2,1)} %up_ref.1, ...), custom_call_target="tpu_custom_call" | custom-call | flops 8321499136 | bytes 48234496 | tf_op jit(solution)/shard_map/forward/pallas_call | solution.py:396
  77.4 0.0 copy-start
  77.4 1.2 %copy-done = bf16[4,4,32,1024]{3,2,1,0:T(8,128)(2,1)S(1)} copy-done((bf16[4,4,32,1024]{3,2,1,0:T(8,128)(2,1)S(1)}, bf16[4,4,32,1024]{3,2,1,0:T(8,128)(2,1)}, u32[]{:S(2)}) %copy-start) | copy-done | bytes 1048600
  78.6 0.0 copy-start.1
  78.6 1.0 %copy-done.1 = bf16[2,2,4,16,1024]{4,3,2,1,0:T(8,128)(2,1)S(1)} copy-done((bf16[2,2,4,16,1024]{4,3,2,1,0:T(8,128)(2,1)S(1)}, bf16[2,2,4,16,1024]{4,3,2,1,0:T(8,128)(2,1)}, u32[]{:S(2)}) %copy-start.1) | copy-done | bytes 524312
  79.6 0.0 copy-start.3
  79.6 0.0 copy-start.2
  79.6 15.0 %decoder_gradient.1 = f32[4096,2048]{1,0:T(8,128)} custom-call(bf16[4,4,32,1024]{3,2,1,0:T(8,128)(2,1)S(1)} %copy-done, bf16[2,128,1024]{2,1,0:T(8,128)(2,1)S(1)} %bitcast.4), custom_call_target="tpu_custom_call" | custom-call | flops 2147483648 | bytes 33554432 | tf_op jit(solution)/shard_map/decoder_gradient/pallas_call | solution.py:456
  94.7 0.0 copy-done.3
  94.7 0.7 copy.15
  95.4 0.0 copy-done.2
  95.4 0.8 copy.16
Async XLA Ops:
  77.4 1.2 %copy-start = (bf16[4,4,32,1024]{3,2,1,0:T(8,128)(2,1)S(1)}, bf16[4,4,32,1024]{3,2,1,0:T(8,128)(2,1)}, u32[]{:S(2)}) copy-start(bf16[4,4,32,1024]{3,2,1,0:T(8,128)(2,1)} %get-tuple-element.9.codes_ref) | copy-start | bytes 3145732
  78.6 1.0 %copy-start.1 = (bf16[2,2,4,16,1024]{4,3,2,1,0:T(8,128)(2,1)S(1)}, bf16[2,2,4,16,1024]{4,3,2,1,0:T(8,128)(2,1)}, u32[]{:S(2)}) copy-start(bf16[2,2,4,16,1024]{4,3,2,1,0:T(8,128)(2,1)} %get-tuple-element.10) | copy-start | bytes 1572868
  79.6 15.0 %copy-start.3 = (bf16[32,4096]{1,0:T(8,128)(2,1)S(1)}, bf16[32,4096]{1,0:T(8,128)(2,1)}, u32[]{:S(2)}) copy-start(bf16[32,4096]{1,0:T(8,128)(2,1)} %get-tuple-element.14) | copy-start | bytes 786436
  79.6 15.7 %copy-start.2 = (f32[32,4096]{1,0:T(8,128)S(1)}, f32[32,4096]{1,0:T(8,128)}, u32[]{:S(2)}) copy-start(f32[32,4096]{1,0:T(8,128)} %get-tuple-element.15) | copy-start | bytes 1572868

commit v2 on v1

--- a/solution.py
+++ b/solution.py
@@ -12,7 +12,7 @@
 BF16 = jnp.bfloat16
 MIB = 1 << 20
 CHUNKS = 4
-HALVES = 2
+QUARTERS = 4
 
 
 def forward(
@@ -26,7 +26,6 @@
     eb_ref,
     dec_hbm,
     db_ref,
-    act_out,
     cg_out,
     codes_out,
     res_out,
@@ -132,21 +131,35 @@
             passed.append(send(here.at[came], here.at[came], dp=partner))
         return passed
 
-    tok_copies = []
-    for i in range(1, dp):
-        peer = lax.rem(d + i, dp)
-        cols = pl.ds(pl.multiple_of(peer * width, 128), width)
-        tok_copies.append(send(tok_ref.at[:, cols], tok_in.at[d], dp=peer))
+    share = width // inner
+    mine = pl.ds(pl.multiple_of(a * share, 128), share)
+    cols = pl.ds(pl.multiple_of(partner * width, 128), width)
+    tok_far = []
+    for i in range(1, pairs):
+        for j in range(2):
+            core_there = lax.rem(c + j, 2)
+            peer = 2 * lax.rem(q + i, pairs) + core_there
+            came = 2 * lax.rem(q + pairs - i, pairs) + core_there
+            there = pl.ds(pl.multiple_of(peer * width + a * share, 128), share)
+            copy = send(tok_ref.at[:, there], tok_in.at[d, :, mine], dp=peer)
+            tok_far.append((came, copy))
+    tok_near = [send(tok_ref.at[:, cols], tok_in.at[d], dp=partner)]
     gate = gate_ref[...].astype(F32)
     hid[d] = (gate / (1.0 + jnp.exp(-gate)) * up_ref[...].astype(F32)).astype(BF16)
     hid_far, hid_near = gather_start(hid)
 
-    pick = (slot_ref[...] == lax.broadcasted_iota(jnp.int32, (rows, rows), 1)).astype(F32)
-    pick = pick.astype(BF16)
-
+    pick = (slot_ref[...] == lax.broadcasted_iota(jnp.int32, (rows, rows), 0)).astype(F32)
+    pick = pick.astype(BF16).T
+
+    for came, copy in tok_far:
+        copy.wait_recv()
+        for i in range(1, inner):
+            piece = tok_in.at[came, :, mine]
+            tok_near.append(send(piece, piece, mp=b * inner + lax.rem(a + i, inner)))
     tok_own.wait()
-    for copy in tok_copies:
+    for copy in tok_near:
         copy.wait_recv()
+    tok_copies = tok_near + [copy for _, copy in tok_far]
     x[...] = jnp.dot(pick, tok_in[...].reshape(rows, width), preferred_element_type=F32).astype(
         BF16
     )
@@ -188,7 +201,6 @@
         codes[k, d] = jnp.maximum(far_sum(k, far_copies) + eb_ref[:, at_chunk(k)], 0.0).astype(
             BF16
         )
-        outs.append(local(codes.at[k, d], act_out.at[:, at_chunk(k)]))
         return gather_start(codes.at[k])
 
     def decode(k, near, passed, cols):
@@ -297,16 +309,15 @@
             for i in range(1, inner)
         ]
 
-    first = [split_sum(s) for s in range(HALVES)]
-    second = [inner_sum(s, first[s]) for s in range(HALVES)]
-    third = [outer_sum(s, second[s]) for s in range(HALVES)]
-    fourth = [inner_gather(s, third[s]) for s in range(HALVES)]
-
+    first = [split_sum(s) for s in range(QUARTERS)]
+    second = [inner_sum(s, first[s]) for s in range(QUARTERS)]
     for k in range(CHUNKS):
         for copy in [core[k]] + far[k]:
             copy.wait_send()
+
     back, back_far = {}, {}
-    for s in range(HALVES):
+
+    def feature_gradient(s):
         for copy in fourth[s]:
             copy.wait_recv()
         outs.append(local(res.at[s], res_out.at[s]))
@@ -324,15 +335,25 @@
                 )
                 if s > 0:
                     value = value + part[k, :, :, cols].reshape(rows, tile)
-                if s < HALVES - 1:
+                if s < QUARTERS - 1:
                     part[k, :, :, cols] = value.reshape(dp, rows_here, tile)
                 else:
                     part_store(k, cols, value)
 
-            if s == HALVES - 1:
+            if s == QUARTERS - 1:
                 back[k] = send(psend.at[k, :, 1 - c], crecv.at[k], dp=partner)
                 if k >= 1:
                     back_far[k - 1] = pair_sum(k - 1, back[k - 1])
+
+    third, fourth = {}, {}
+    for s in range(QUARTERS):
+        third[s] = outer_sum(s, second[s])
+        if s >= 1:
+            fourth[s - 1] = inner_gather(s - 1, third[s - 1])
+    feature_gradient(0)
+    fourth[QUARTERS - 1] = inner_gather(QUARTERS - 1, third[QUARTERS - 1])
+    for s in range(1, QUARTERS):
+        feature_gradient(s)
     back_far[last] = pair_sum(last, back[last])
     for k in range(CHUNKS):
         cg_out[:, at_chunk(k)] = far_sum(k, back_far[k])
@@ -342,25 +363,22 @@
     for k in range(CHUNKS):
         for copy in gathers[k][0] + [gathers[k][1]] + passes[k] + [back[k]] + back_far[k]:
             copy.wait_send()
-    for s in range(HALVES):
+    for s in range(QUARTERS):
         for copy in first[s] + second[s] + third[s] + fourth[s]:
             copy.wait_send()
     for copy in outs:
         copy.wait()
 
 
-def decoder_gradient(scale, codes_ref, res_ref, out_ref):
+def decoder_gradient(scale, codes_ref, res_ref, cg_ref, act_out, cg_out, out_ref):
     rows = codes_ref.shape[0] * codes_ref.shape[1]
     columns = res_ref.shape[2]
+    act_out[...] = codes_ref[lax.axis_index("dp")]
+    cg_out[...] = cg_ref[...]
+    codes = codes_ref[...].reshape(rows, codes_ref.shape[2]).T
     for s in range(res_ref.shape[0]):
         out_ref[:, s * columns : (s + 1) * columns] = (
-            lax.dot_general(
-                codes_ref[...].reshape(rows, codes_ref.shape[2]),
-                res_ref[s],
-                (((0,), (0,)), ((), ())),
-                preferred_element_type=F32,
-            )
-            * scale
+            jnp.dot(codes, res_ref[s], preferred_element_type=F32) * scale
         )
 
 
@@ -385,26 +403,25 @@
     inner = 1 << ((mp.bit_length() - 1) // 2)
     outer = mp // inner
     r16 = rows // mp
-    cw, sw = features // CHUNKS, width // HALVES
+    cw, sw = features // CHUNKS, width // QUARTERS
     tile, stile = min(256, cw, width), min(256, sw)
     far = max(pairs - 1, 1)
-    copies = (dp - 1) + 2 * pairs - 1 + CHUNKS * (1 + pairs - 1 + 2 * pairs - 1)
-    copies += HALVES * 2 * (inner - 1 + outer - 1) + CHUNKS * pairs
-    locals_ = 1 + CHUNKS + 1 + CHUNKS + 2 * CHUNKS + HALVES
+    copies = (dp - 1) + 2 * (pairs - 1) * (inner - 1) + 2 * pairs - 1 + CHUNKS * (1 + pairs - 1 + 2 * pairs - 1)
+    copies += QUARTERS * 2 * (inner - 1 + outer - 1) + CHUNKS * pairs
+    locals_ = 1 + CHUNKS + 1 + CHUNKS + CHUNKS + QUARTERS
     vmem = pl.BlockSpec(memory_space=pltpu.VMEM)
     anywhere = pl.BlockSpec(memory_space=pl.ANY)
-    local_codes, code_grad, codes, res = pl.pallas_call(
+    code_grad, codes, res = pl.pallas_call(
         functools.partial(
             forward, (dp, pairs, inner, outer, rows_here, cw, sw, tile, stile)
         ),
         out_shape=(
-            jax.ShapeDtypeStruct((rows_here, features), BF16),
             jax.ShapeDtypeStruct((rows_here, features), F32),
             jax.ShapeDtypeStruct((CHUNKS, dp, rows_here, cw), BF16),
-            jax.ShapeDtypeStruct((HALVES, inner, outer, r16, sw), BF16),
+            jax.ShapeDtypeStruct((QUARTERS, inner, outer, r16, sw), BF16),
         ),
         in_specs=[vmem, anywhere, vmem, vmem, anywhere, anywhere, vmem, anywhere, vmem],
-        out_specs=(anywhere, vmem, anywhere, anywhere),
+        out_specs=(vmem, anywhere, anywhere),
         scratch_shapes=[
             pltpu.VMEM((CHUNKS, width, cw), BF16),
             pltpu.VMEM((features, width), BF16),
@@ -420,12 +437,12 @@
             pltpu.VMEM((CHUNKS, far, rows_here, cw), BF16),
             pltpu.VMEM((CHUNKS, dp, rows_here, cw), BF16),
             pltpu.VMEM((rows, width), F32),
-            pltpu.VMEM((HALVES, inner, outer, r16, sw), BF16),
-            pltpu.VMEM((HALVES, max(inner - 1, 1), outer, r16, sw), BF16),
-            pltpu.VMEM((HALVES, outer, r16, sw), F32),
-            pltpu.VMEM((HALVES, outer, r16, sw), BF16),
-            pltpu.VMEM((HALVES, max(outer - 1, 1), r16, sw), BF16),
-            pltpu.VMEM((HALVES, inner, outer, r16, sw), BF16),
+            pltpu.VMEM((QUARTERS, inner, outer, r16, sw), BF16),
+            pltpu.VMEM((QUARTERS, max(inner - 1, 1), outer, r16, sw), BF16),
+            pltpu.VMEM((QUARTERS, outer, r16, sw), F32),
+            pltpu.VMEM((QUARTERS, outer, r16, sw), BF16),
+            pltpu.VMEM((QUARTERS, max(outer - 1, 1), r16, sw), BF16),
+            pltpu.VMEM((QUARTERS, inner, outer, r16, sw), BF16),
             pltpu.SemaphoreType.DMA((copies,)),
             pltpu.SemaphoreType.DMA((copies,)),
             pltpu.SemaphoreType.DMA((locals_,)),
@@ -440,7 +457,7 @@
         ),
         name="forward",
     )(
-        slot_source.reshape(rows, 1),
+        slot_source.reshape(1, rows),
         tokens_in,
         gate_pre,
         up_pre,
@@ -453,24 +470,29 @@
 
     block = min(256, cw)
     per = cw // block
-    decoder_grad = pl.pallas_call(
+    here = pl.BlockSpec((rows_here, block), lambda f: (0, f))
+    return pl.pallas_call(
         functools.partial(decoder_gradient, 1.0 / rows_here),
         grid=(features // block,),
-        out_shape=jax.ShapeDtypeStruct((features, width), F32),
+        out_shape=(
+            jax.ShapeDtypeStruct((rows_here, features), BF16),
+            jax.ShapeDtypeStruct((rows_here, features), F32),
+            jax.ShapeDtypeStruct((features, width), F32),
+        ),
         in_specs=[
             pl.BlockSpec((None, dp, rows_here, block), lambda f: (f // per, 0, 0, f % per)),
-            pl.BlockSpec((HALVES, rows, sw), lambda f: (0, 0, 0)),
+            pl.BlockSpec((QUARTERS, rows, sw), lambda f: (0, 0, 0)),
+            here,
         ],
-        out_specs=pl.BlockSpec((block, width), lambda f: (f, 0)),
-        compiler_params=pltpu.CompilerParams(vmem_limit_bytes=32 * MIB),
+        out_specs=(here, here, pl.BlockSpec((block, width), lambda f: (f, 0))),
+        compiler_params=pltpu.CompilerParams(vmem_limit_bytes=62 * MIB),
         cost_estimate=pl.CostEstimate(
             flops=2 * rows * width * features,
             bytes_accessed=4 * width * features,
             transcendentals=0,
         ),
         name="decoder_gradient",
-    )(codes, res.reshape(HALVES, rows, sw))
-    return (local_codes, code_grad, decoder_grad)
+    )(codes, res.reshape(QUARTERS, rows, sw), code_grad)
 
 
 def solution(mesh):

time: 96.4 us -> 98.4 us (1.021)
  Pallas kernels: 90.4 us -> 96.8 us
  local copies, waits for them, and re-layouts: 5.15 us -> 0 us
    pallas_call x1, Pallas kernels: 75.3 us -> 80.4 us  [on_device(): pl.pallas_call(functools.partial(forward, (dp, pairs, inner, outer, rows_...]
    unnamed x10 -> x0, local copies, waits for them, and re-layouts: 3.76 us -> none
    reshape x1 -> x0, local copies, waits for them, and re-layouts: 1.39 us -> none  [on_device(): slot_source.reshape(rows, 1)]
    pallas_call x1, Pallas kernels: 15 us -> 16.4 us  [on_device(): pl.pallas_call(functools.partial(decoder_gradient, 1.0 / rows_here), grid...]
where the time goes in v2:
time: 98.4 us; the launch traced here: 97.5 us
  Pallas kernels  96.8 us (98%)
    pallas_call x1, Pallas kernels, on_device(): pl.pallas_call(functools.partial(forward, (dp, pairs, inner, outer, rows_...  80.4 us
    pallas_call x1, Pallas kernels, on_device(): pl.pallas_call(functools.partial(decoder_gradient, 1.0 / rows_here), grid...  16.4 us

profile of v2, /device:TPU:0, one launch (start us, length us, event | category | flops | bytes accessed | tf_op | source)
XLA Modules:
  0.0 97.5 jit_solution(4547508747418329220)
XLA Ops:
  0.6 80.4 %forward.1 = (f32[32,4096]{1,0:T(8,128)}, bf16[4,4,32,1024]{3,2,1,0:T(8,128)(2,1)}, bf16[4,2,4,16,512]{4,3,2,1,0:T(8,128)(2,1)}) custom-call(s32[1,128]{1,0:T(1,128)} %bitcast.6, bf16[32,8192]{1,0:T(8,128)(2,1)} %tok_ref.1, bf16[32,3584]{1,0:T(8,128)(2,1)} %gate_ref.1, bf16[32,3584]{1,0:T(8,128)(2,1)} %up_ref.1, bf16[3584,2048]{1,0:T(8,128)(2,1)} %down_hbm.1, ...), custom_call_target="tpu_custom_call" | custom-call | flops 8321499136 | bytes 48234496 | tf_op jit(solution)/shard_map/forward/pallas_call | solution.py:414
  81.1 16.4 %decoder_gradient.1 = (bf16[32,4096]{1,0:T(8,128)(2,1)}, f32[32,4096]{1,0:T(8,128)}, f32[4096,2048]{1,0:T(8,128)}) custom-call(bf16[4,4,32,1024]{3,2,1,0:T(8,128)(2,1)} %get-tuple-element.6.codes_ref, bf16[4,128,512]{2,1,0:T(8,128)(2,1)} %bitcast.7, f32[32,4096]{1,0:T(8,128)} %get-tuple-element.8.cg_ref), custom_call_target="tpu_custom_call" | custom-call | flops 2147483648 | bytes 33554432 | tf_op jit(solution)/shard_map/decoder_gradient/pallas_call | solution.py:474
